TPU v7x, 32 devices: a whole 2x2x4 slice. The times are simulated.
32 devices in a mesh: dp: 16 (over z, y, core), tensor: 2 (over x).
Axes of the slice: x: 2, y: 2, z: 4, core: 2. Of those that a mesh axis runs over, the one named last changes fastest.
Arguments:
- tokens: bfloat16 [24576, 640], P('dp'), may hold values from -6 to 6
- w_query: bfloat16 [640, 1024], P(None, 'tensor'), may hold values from -0.25 to 0.25
- w_key: bfloat16 [640, 256], replicated, may hold values from -0.25 to 0.25
- w_value: bfloat16 [640, 256], replicated, may hold values from -0.25 to 0.25
- w_output: bfloat16 [1024, 640], P('tensor'), may hold values from -0.1875 to 0.1875
- w_gate: bfloat16 [640, 2048], P(None, 'tensor'), may hold values from -0.25 to 0.25
- w_up: bfloat16 [640, 2048], P(None, 'tensor'), may hold values from -0.25 to 0.25
- w_down: bfloat16 [2048, 640], P('tensor'), may hold values from -0.125 to 0.125
- gain_input: float32 [640], replicated, may hold values from -0.4 to 0.6
- gain_query: float32 [256], replicated, may hold values from -0.4 to 0.6
- gain_key: float32 [256], replicated, may hold values from -0.4 to 0.6
- gain_post_attn: float32 [640], replicated, may hold values from -0.4 to 0.6
- gain_pre_ffn: float32 [640], replicated, may hold values from -0.4 to 0.6
- gain_post_ffn: float32 [640], replicated, may hold values from -0.4 to 0.6
- out_grad: bfloat16 [24576, 640], P('dp'), may hold values from -6 to 6
- lengths: int32 [24], replicated, may hold values from 1 to 1536, as said below
- holder: int32 [24], replicated, may hold values from 0 to 15
Outputs:
- layer_out: float32 [24576, 640], P('dp')
- tokens_grad: float32 [24576, 640], P('dp')
- grad_w_query: float32 [640, 1024], P(None, 'tensor')
- grad_w_key: float32 [640, 256], replicated
- grad_w_value: float32 [640, 256], replicated
- grad_w_output: float32 [1024, 640], P('tensor')
- grad_w_gate: float32 [640, 2048], P(None, 'tensor')
- grad_w_up: float32 [640, 2048], P(None, 'tensor')
- grad_w_down: float32 [2048, 640], P('tensor')
- grad_gain_input: float32 [640], replicated
- grad_gain_query: float32 [256], replicated
- grad_gain_key: float32 [256], replicated
- grad_gain_post_attn: float32 [640], replicated
- grad_gain_pre_ffn: float32 [640], replicated
- grad_gain_post_ffn: float32 [640], replicated
Inputs may be any that keep to these rules, and one draw needn't show every extreme that they name: The sequences of one index d of dp (holder = d) have lengths summing to at most 1536; one sequence has exactly 1536 tokens; an index of dp holds 0 to 3 sequences.
All inputs are finite; a program needn't handle non-finite values.
Results may differ from a plain program's by a relative error of at most 0.015.
Values sent between devices are 32-bit elements; how exact they have to be, the bound alone decides.
A program may use at most 192 MiB of HBM per device.

v0:
```python
import jax
import jax.numpy as jnp
from jax import lax
from jax.sharding import PartitionSpec as P

HD = 256
EPS = 1e-06
THETA = 1000000.0


def layout(lengths, holder, device, tok_rows):
    seq_count = lengths.shape[0]
    owned_mask = holder == device
    local_len = jnp.where(owned_mask, lengths, 0)
    starts = jnp.cumsum(local_len) - local_len
    row_ids = jnp.arange(tok_rows, dtype=jnp.int32)[:, None]
    inside = (
        owned_mask[None, :]
        & (row_ids >= starts[None, :])
        & (row_ids < (starts + local_len)[None, :])
    )
    inside_int = inside.astype(jnp.int32)
    segment = (
        jnp.sum(inside_int * (jnp.arange(seq_count, dtype=jnp.int32)[None, :] + 1), axis=1) - 1
    )
    position = jnp.sum(inside_int * (row_ids - starts[None, :]), axis=1)
    return (segment, position)


def rotary_tables(position):
    half_width = HD // 2
    frequency = THETA ** (-(2.0 * jnp.arange(half_width, dtype=jnp.float32)) / HD)
    angles = position.astype(jnp.float32)[:, None] * frequency[None, :]
    angles = jnp.concatenate([angles, angles], axis=1)
    return (jnp.cos(angles), jnp.sin(angles))


def rotate(vectors, cosine, sine):
    half_width = vectors.shape[-1] // 2
    turned = jnp.concatenate([-vectors[..., half_width:], vectors[..., :half_width]], axis=-1)
    return vectors * cosine + turned * sine


def unrotate(grads_in, cosine, sine):
    half_width = grads_in.shape[-1] // 2
    weighted = grads_in * sine
    turned = jnp.concatenate([weighted[..., half_width:], -weighted[..., :half_width]], axis=-1)
    return grads_in * cosine + turned


def norm_forward(vectors, scaling):
    inverse = lax.rsqrt(jnp.mean(vectors * vectors, axis=-1, keepdims=True) + EPS)
    plain = vectors * inverse
    return (plain * (1.0 + scaling), plain, inverse)


def norm_backward(grads_in, plain, inverse, scaling):
    scaled = grads_in * (1.0 + scaling)
    grads_out = inverse * (scaled - plain * jnp.mean(scaled * plain, axis=-1, keepdims=True))
    gain_grad = jnp.sum(grads_in * plain, axis=tuple(range(grads_in.ndim - 1)))
    return (grads_out, gain_grad)


def left_dot(first, second):
    return lax.dot_general(
        first, second, (((0,), (0,)), ((), ())), preferred_element_type=jnp.float32
    )


def right_dot(first, second):
    return lax.dot_general(
        first, second, (((1,), (1,)), ((), ())), preferred_element_type=jnp.float32
    )


def left_full(first, second):
    return lax.dot_general(
        first,
        second,
        (((0,), (0,)), ((), ())),
        precision=lax.Precision.HIGHEST,
        preferred_element_type=jnp.float32,
    )


def right_full(first, second):
    return lax.dot_general(
        first,
        second,
        (((1,), (1,)), ((), ())),
        precision=lax.Precision.HIGHEST,
        preferred_element_type=jnp.float32,
    )


def gelu_tanh(vectors):
    return jax.nn.gelu(vectors, approximate=True)


def block_scores(query_block, key_states, segment, first_row, score_scale):
    block_rows = query_block.shape[0]
    total_rows = key_states.shape[0]
    row_ids = first_row + jnp.arange(block_rows, dtype=jnp.int32)
    column_ids = jnp.arange(total_rows, dtype=jnp.int32)
    seg_rows = lax.dynamic_slice_in_dim(segment, first_row, block_rows)
    allowed = (seg_rows[:, None] == segment[None, :]) & (seg_rows[:, None] >= 0) & (
        column_ids[None, :] <= row_ids[:, None]
    ) | (column_ids[None, :] == row_ids[:, None])
    raw_scores = (
        jnp.einsum("qhd,kd->hqk", query_block, key_states, preferred_element_type=jnp.float32)
        * score_scale
    )
    return jnp.where(allowed[None, :, :], raw_scores, -1e30)


def local(
    tokens,
    w_query,
    w_key,
    w_value,
    w_output,
    w_gate,
    w_up,
    w_down,
    gain_input,
    gain_query,
    gain_key,
    gain_post_attn,
    gain_pre_ffn,
    gain_post_ffn,
    out_grad,
    lengths,
    holder,
):
    tok_rows = tokens.shape[0]
    local_heads = w_query.shape[1] // HD
    score_scale = HD ** (-0.5)
    device = lax.axis_index("dp")
    segment, position = layout(lengths, holder, device, tok_rows)
    cosine, sine = rotary_tables(position)
    block_rows = min(512, tok_rows)
    block_count = tok_rows // block_rows
    first_rows = jnp.arange(block_count, dtype=jnp.int32) * block_rows
    source = tokens.astype(jnp.float32)
    normed, normed_plain, normed_inverse = norm_forward(source, gain_input)
    normed_low = normed.astype(jnp.bfloat16)
    query_pre = jnp.dot(normed_low, w_query, preferred_element_type=jnp.float32).reshape(
        tok_rows, local_heads, HD
    )
    key_pre = jnp.dot(normed_low, w_key, preferred_element_type=jnp.float32)
    value_pre = jnp.dot(normed_low, w_value, preferred_element_type=jnp.float32)
    query_normed, query_plain, query_inverse = norm_forward(query_pre, gain_query)
    query_states = rotate(query_normed, cosine[:, None, :], sine[:, None, :]).astype(jnp.bfloat16)
    key_normed, key_plain, key_inverse = norm_forward(key_pre, gain_key)
    key_states = rotate(key_normed, cosine, sine).astype(jnp.bfloat16)
    value_states = value_pre.astype(jnp.bfloat16)
    query_blocks = query_states.reshape(block_count, block_rows, local_heads, HD)

    def forward_block(inputs):
        query_block, first_row = inputs
        scores = block_scores(query_block, key_states, segment, first_row, score_scale)
        row_max = jnp.max(scores, axis=-1, keepdims=True)
        exponent = jnp.exp(scores - row_max)
        row_total = jnp.sum(exponent, axis=-1, keepdims=True)
        attn_probs = exponent / row_total
        mixed_block = jnp.einsum(
            "hqk,kd->qhd",
            attn_probs.astype(jnp.bfloat16),
            value_states,
            preferred_element_type=jnp.float32,
        )
        return (mixed_block, (row_max + jnp.log(row_total))[..., 0])

    mixed_blocks, log_totals = lax.map(forward_block, (query_blocks, first_rows))
    mixed_heads = mixed_blocks.reshape(tok_rows, local_heads * HD).astype(jnp.bfloat16)
    branch = lax.psum(jnp.dot(mixed_heads, w_output, preferred_element_type=jnp.float32), "tensor")
    post_attn, post_attn_plain, post_attn_inverse = norm_forward(branch, gain_post_attn)
    middle = source + post_attn
    normed2, normed2_plain, normed2_inverse = norm_forward(middle, gain_pre_ffn)
    normed2_low = normed2.astype(jnp.bfloat16)
    gate_proj = jnp.dot(normed2_low, w_gate, preferred_element_type=jnp.float32)
    up_proj = jnp.dot(normed2_low, w_up, preferred_element_type=jnp.float32)
    activation, gelu_pull = jax.vjp(gelu_tanh, gate_proj)
    hidden = (activation * up_proj).astype(jnp.bfloat16)
    ffn_sum = lax.psum(jnp.dot(hidden, w_down, preferred_element_type=jnp.float32), "tensor")
    post_ffn, post_ffn_plain, post_ffn_inverse = norm_forward(ffn_sum, gain_post_ffn)
    layer_out = middle + post_ffn
    valid = (segment >= 0).astype(jnp.float32)[:, None]
    upstream = out_grad.astype(jnp.float32) * valid
    grad_ffn, grad_post_ffn = norm_backward(
        upstream, post_ffn_plain, post_ffn_inverse, gain_post_ffn
    )
    grad_ffn_low = grad_ffn.astype(jnp.bfloat16)
    grad_down = left_dot(hidden, grad_ffn_low)
    grad_hidden = right_dot(grad_ffn_low, w_down)
    grad_gate_low = gelu_pull(grad_hidden * up_proj)[0].astype(jnp.bfloat16)
    grad_up_low = (grad_hidden * activation).astype(jnp.bfloat16)
    grad_gate = left_dot(normed2_low, grad_gate_low)
    grad_up = left_dot(normed2_low, grad_up_low)
    grad_normed2 = lax.psum(
        right_dot(grad_gate_low, w_gate) + right_dot(grad_up_low, w_up), "tensor"
    )
    grad_pre_part, grad_pre_ffn = norm_backward(
        grad_normed2, normed2_plain, normed2_inverse, gain_pre_ffn
    )
    grad_middle = upstream + grad_pre_part
    grad_branch, grad_post_attn = norm_backward(
        grad_middle, post_attn_plain, post_attn_inverse, gain_post_attn
    )
    grad_branch_low = grad_branch.astype(jnp.bfloat16)
    grad_output = left_dot(mixed_heads, grad_branch_low)
    grad_mixed = (
        right_dot(grad_branch_low, w_output)
        .astype(jnp.bfloat16)
        .reshape(block_count, block_rows, local_heads, HD)
    )

    def backward_block(sums_carry, inputs):
        key_sum, value_sum = sums_carry
        query_block, mixed_grad_block, total_block, first_row = inputs
        scores = block_scores(query_block, key_states, segment, first_row, score_scale)
        attn_probs = jnp.exp(scores - total_block[..., None])
        grad_probs = jnp.einsum(
            "qhd,kd->hqk", mixed_grad_block, value_states, preferred_element_type=jnp.float32
        )
        grad_scores = (
            attn_probs
            * (grad_probs - jnp.sum(attn_probs * grad_probs, axis=-1, keepdims=True))
            * score_scale
        ).astype(jnp.bfloat16)
        query_grad_block = jnp.einsum(
            "hqk,kd->qhd", grad_scores, key_states, preferred_element_type=jnp.float32
        )
        key_sum = key_sum + jnp.einsum(
            "hqk,qhd->kd", grad_scores, query_block, preferred_element_type=jnp.float32
        )
        value_sum = value_sum + jnp.einsum(
            "hqk,qhd->kd",
            attn_probs.astype(jnp.bfloat16),
            mixed_grad_block,
            preferred_element_type=jnp.float32,
        )
        return ((key_sum, value_sum), query_grad_block)

    zeroes = jnp.zeros((tok_rows, HD), jnp.float32)
    (grad_keys_part, grad_values_part), query_grad_blocks = lax.scan(
        backward_block, (zeroes, zeroes), (query_blocks, grad_mixed, log_totals, first_rows)
    )
    grad_queries = query_grad_blocks.reshape(tok_rows, local_heads, HD)
    grad_query_pre, grad_gain_query_part = norm_backward(
        unrotate(grad_queries, cosine[:, None, :], sine[:, None, :]),
        query_plain,
        query_inverse,
        gain_query,
    )
    grad_query_low = grad_query_pre.astype(jnp.bfloat16).reshape(tok_rows, local_heads * HD)
    grad_query = left_dot(normed_low, grad_query_low)
    normed_wide = normed_low.astype(jnp.float32)
    w_key_wide = w_key.astype(jnp.float32)
    w_value_wide = w_value.astype(jnp.float32)
    grad_keys, grad_values, from_query, grad_gain_query = lax.psum(
        (
            grad_keys_part,
            grad_values_part,
            right_dot(grad_query_low, w_query),
            grad_gain_query_part,
        ),
        "tensor",
    )
    grad_key_pre, grad_gain_key_local = norm_backward(
        unrotate(grad_keys, cosine, sine), key_plain, key_inverse, gain_key
    )
    grad_key_local = left_full(normed_wide, grad_key_pre)
    grad_value_local = left_full(normed_wide, grad_values)
    grad_normed = (
        from_query + right_full(grad_key_pre, w_key_wide) + right_full(grad_values, w_value_wide)
    )
    grad_key, grad_value, grad_gain_key = lax.psum(
        (grad_key_local, grad_value_local, grad_gain_key_local), "dp"
    )
    grad_input_part, grad_gain_input = norm_backward(
        grad_normed, normed_plain, normed_inverse, gain_input
    )
    tokens_grad = grad_middle + grad_input_part
    all_summed = (
        lax.psum_scatter(grad_query, "dp", scatter_dimension=0, tiled=True),
        lax.psum_scatter(grad_output, "dp", scatter_dimension=0, tiled=True),
        lax.psum_scatter(grad_gate, "dp", scatter_dimension=0, tiled=True),
        lax.psum_scatter(grad_up, "dp", scatter_dimension=0, tiled=True),
        lax.psum_scatter(grad_down, "dp", scatter_dimension=0, tiled=True),
        lax.psum_scatter(grad_gain_input, "dp", scatter_dimension=0, tiled=True),
        lax.psum_scatter(grad_gain_query, "dp", scatter_dimension=0, tiled=True),
        lax.psum_scatter(grad_post_attn, "dp", scatter_dimension=0, tiled=True),
        lax.psum_scatter(grad_pre_ffn, "dp", scatter_dimension=0, tiled=True),
        lax.psum_scatter(grad_post_ffn, "dp", scatter_dimension=0, tiled=True),
    )
    all_full = (
        lax.all_gather(all_summed[0], "dp", axis=0, tiled=True),
        lax.all_gather(all_summed[1], "dp", axis=0, tiled=True),
        lax.all_gather(all_summed[2], "dp", axis=0, tiled=True),
        lax.all_gather(all_summed[3], "dp", axis=0, tiled=True),
        lax.all_gather(all_summed[4], "dp", axis=0, tiled=True),
        lax.all_gather(all_summed[5], "dp", axis=0, tiled=True),
        lax.all_gather(all_summed[6], "dp", axis=0, tiled=True),
        lax.all_gather(all_summed[7], "dp", axis=0, tiled=True),
        lax.all_gather(all_summed[8], "dp", axis=0, tiled=True),
        lax.all_gather(all_summed[9], "dp", axis=0, tiled=True),
    )
    return (
        layer_out,
        tokens_grad,
        all_full[0],
        grad_key,
        grad_value,
        all_full[1],
        all_full[2],
        all_full[3],
        all_full[4],
        all_full[5],
        all_full[6],
        grad_gain_key,
        all_full[7],
        all_full[8],
        all_full[9],
    )


def solution(mesh):
    return jax.shard_map(
        local,
        mesh=mesh,
        in_specs=(
            P("dp", None),
            P(None, "tensor"),
            P(),
            P(),
            P("tensor", None),
            P(None, "tensor"),
            P(None, "tensor"),
            P("tensor", None),
            P(),
            P(),
            P(),
            P(),
            P(),
            P(),
            P("dp", None),
            P(),
            P(),
        ),
        out_specs=(
            P("dp", None),
            P("dp", None),
            P(None, "tensor"),
            P(),
            P(),
            P("tensor", None),
            P(None, "tensor"),
            P(None, "tensor"),
            P("tensor", None),
            P(),
            P(),
            P(),
            P(),
            P(),
            P(),
        ),
        check_vma=False,
    )
```

profile of v0, /device:TPU:0, one launch (start us, length us, event | category | flops | bytes accessed | tf_op | source)
XLA Modules:
  0.0 1547.5 jit_solution(16992179626408646211)
XLA Ops:
  69.3 39.3 %while.29 = (s32[]{:T(128)}, bf16[3,512,2,256]{3,1,2,0:T(8,128)(2,1)}, f32[3,2,512]{2,1,0:T(2,128)S(1)}, s32[3]{0:T(128)S(1)}, s32[1536]{0:T(1024)S(1)}, /*index...) while((s32[]{:T(128)}, ...), condition=%wide.region_9.10_spmd.clone, body=%wide.region_6.9_spmd.sunk.clone | while | flops 1634205696 | bytes 40944880 | solution.py:174
  117.3 105.1 %all-reduce.20.cloned.1.call-done = f32[1536,640]{1,0:T(8,128)} async-done(((f32[1536,640]{1,0:T(8,128)}), f32[1536,640]{1,0:T(8,128)}) %all-reduce.20.cloned.1.call-update) | async-done | bytes 3932176 | tf_op jit(solution)/shard_map/psum | solution.py:176
  244.9 102.4 %all-reduce.22.cloned.1.call-done = f32[1536,640]{1,0:T(8,128)} async-done(((f32[1536,640]{1,0:T(8,128)}), f32[1536,640]{1,0:T(8,128)}) %all-reduce.22.cloned.1.call-update) | async-done | bytes 3932176 | tf_op jit(solution)/shard_map/psum | solution.py:185
  375.6 100.0 %all-reduce.24.cloned.1.call-done = f32[1536,640]{1,0:T(8,128)} async-done(((f32[1536,640]{1,0:T(8,128)}), f32[1536,640]{1,0:T(8,128)}) %all-reduce.24.cloned.1.call-update) | async-done | bytes 3932176 | tf_op jit(solution)/shard_map/psum | solution.py:200
  499.8 116.4 %while.30 = (s32[]{:T(128)}, f32[1536,256]{1,0:T(8,128)}, f32[1536,256]{1,0:T(8,128)S(1)}, f32[3,512,2,256]{3,1,2,0:T(8,128)}, s32[3]{0:T(128)S(1)}, /*index=5*/...) while((s32[]{:T(128)}, f32[1536,256]{1,0:T(8,128)}, ...), condition=%wide.region_21.22_spmd.clone.clone, body=%wide.region_19.21_spmd.clone.sunk.clone | while | flops 4054849536 | bytes 115111200 | solution.py:246
  515.6 12.1 fusion.188
  527.7 10.6 fusion.190
  554.1 12.5 fusion.188
  593.0 12.5 fusion.188
  605.5 10.7 fusion.190
  632.9 22.3 %multiply_reduce_fusion.9 = (f32[256]{0:T(256)S(1)}, f32[3,512,2]{2,1,0:T(8,128)S(1)}) fusion(f32[3,512,2,256]{3,2,1,0:T(2,128)S(1)} %copy-done.14, f32[3,512,2]{2,1,0:T(8,128)S(1)} %bitcast.271, f32[256]{0:T(256)S(1)} %broadcast_add_fusion.6, f32[3,512,2,128]{3,2,1,0:T(2,128)S(1)} %copy.137, f32[3,512,2,128]{3,2,1,0:T(2,128)S(1)} %copy.136, ...), kind=kLoop, calls=%fused_computation.124 | loop fusion | flops 7074560 | bytes 11036672 | tf_op jit(solution)/shard_map/reduce_sum | solution.py:60
  696.4 49.6 %reduce-scatter.6.cloned.1.call-done = f32[40,512]{1,0:T(8,128)} async-done(((f32[640,512]{1,0:T(8,128)}), f32[40,512]{1,0:T(8,128)}) %reduce-scatter.6.cloned.1.call-update) | async-done | bytes 81936 | tf_op jit(solution)/shard_map/reduce_scatter | solution.py:286
  746.1 67.4 %reduce-scatter.14.cloned.1.call-done = f32[64,640]{1,0:T(8,128)} async-done(((f32[1024,640]{1,0:T(8,128)}), f32[64,640]{1,0:T(8,128)}) %reduce-scatter.14.cloned.1.call-update) | async-done | bytes 163856 | tf_op jit(solution)/shard_map/reduce_scatter | solution.py:290
  813.6 67.7 %reduce-scatter.12.cloned.1.call-done = f32[40,1024]{1,0:T(8,128)} async-done(((f32[640,1024]{1,0:T(8,128)}), f32[40,1024]{1,0:T(8,128)}) %reduce-scatter.12.cloned.1.call-update) | async-done | bytes 163856 | tf_op jit(solution)/shard_map/reduce_scatter | solution.py:289
  881.3 67.6 %reduce-scatter.10.cloned.1.call-done = f32[40,1024]{1,0:T(8,128)} async-done(((f32[640,1024]{1,0:T(8,128)}), f32[40,1024]{1,0:T(8,128)}) %reduce-scatter.10.cloned.1.call-update) | async-done | bytes 163856 | tf_op jit(solution)/shard_map/reduce_scatter | solution.py:288
  960.6 28.7 %all-gather.8.cloned.1.call-done = f32[512,640]{1,0:T(8,128)} async-done(((f32[32,640]{1,0:T(8,128)}), f32[512,640]{1,0:T(8,128)}) %all-gather.8.cloned.1.call-update) | async-done | bytes 1310736 | tf_op jit(solution)/shard_map/all_gather | solution.py:299
  989.4 40.0 %all-gather.6.cloned.1.call-done = f32[640,512]{1,0:T(8,128)} async-done(((f32[40,512]{1,0:T(8,128)}), f32[640,512]{1,0:T(8,128)}) %all-gather.6.cloned.1.call-update) | async-done | bytes 1310736 | tf_op jit(solution)/shard_map/all_gather | solution.py:298
  1029.4 44.6 %all-gather.14.cloned.1.call-done = f32[1024,640]{1,0:T(8,128)} async-done(((f32[64,640]{1,0:T(8,128)}), f32[1024,640]{1,0:T(8,128)}) %all-gather.14.cloned.1.call-update) | async-done | bytes 2621456 | tf_op jit(solution)/shard_map/all_gather | solution.py:302
  1074.0 44.3 %all-gather.12.cloned.1.call-done = f32[640,1024]{1,0:T(8,128)} async-done(((f32[40,1024]{1,0:T(8,128)}), f32[640,1024]{1,0:T(8,128)}) %all-gather.12.cloned.1.call-update) | async-done | bytes 2621456 | tf_op jit(solution)/shard_map/all_gather | solution.py:301
  1118.3 44.4 %all-gather.10.cloned.1.call-done = f32[640,1024]{1,0:T(8,128)} async-done(((f32[40,1024]{1,0:T(8,128)}), f32[640,1024]{1,0:T(8,128)}) %all-gather.10.cloned.1.call-update) | async-done | bytes 2621456 | tf_op jit(solution)/shard_map/all_gather | solution.py:300
  1162.7 172.9 %all-reduce.28.cloned.1.call-done = (f32[1536,640]{1,0:T(8,128)}, f32[1536,256]{0,1:T(8,128)}, f32[1536,256]{1,0:T(8,128)}) async-done(((f32[1536,640]{1,0:T(8,128)}, f32[1536,256]{0,1:T(8,128)}, f32[1536,256]{1,0:T(8,128)}), (f32[1536,640]{1,0:T(8,128)}, f32[1536,256]{0,1:T(8,128)}, f32[1536,256]{1,0:T(8,128)})) %all-reduce.28.cloned.1.call-update) | async-done | bytes 7077904 | tf_op jit(solution)/shard_map/psum | solution.py:261
  1370.8 61.2 %all-reduce.11 = (f32[640]{0:T(1024)S(1)}, f32[256]{0:T(256)S(1)}, f32[640]{0:T(1024)S(1)}, f32[640]{0:T(1024)S(1)}, f32[640]{0:T(1024)S(1)}) all-reduce(f32[640]{0:T(1024)S(1)} %get-tuple-element.261, f32[256]{0:T(256)S(1)} %get-tuple-element.257, ...), channel_id=7, replica_groups=mesh['dp'=16,'tensor'=2] {'dp'}, use_global_device_ids=true, to_apply=%region_36.37.clone | all-reduce | flops 2816 | bytes 22528
  1437.9 58.1 %all-reduce.10 = (f32[640]{0:T(1024)}, f32[256]{0:T(256)}, f32[256]{0:T(256)}, f32[640]{0:T(1024)}, f32[640]{0:T(1024)}, /*index=5*/f32[640]{0:T(1024)}) all-reduce(f32[640]{0:T(1024)S(1)} %dynamic-slice_dynamic-update-slice_fusion.3, f32[256]{0:T(256)S(1)} %dynamic-update-slice.1, ...), channel_id=1, replica_groups=mesh['dp'=16,'tensor'=2] {'dp'}, use_global_device_ids=true, to_apply=%add | all-reduce | flops 3072 | bytes 24576
  1501.2 26.2 %all-reduce.26.cloned.1.call-done = (f32[640,256]{1,0:T(8,128)}, f32[640,256]{1,0:T(8,128)}) async-done(((f32[640,256]{1,0:T(8,128)}, f32[640,256]{1,0:T(8,128)}), (f32[640,256]{1,0:T(8,128)}, f32[640,256]{1,0:T(8,128)})) %all-reduce.26.cloned.1.call-update) | async-done | bytes 1310736 | tf_op jit(solution)/shard_map/psum | solution.py:278
  (391 shorter events, 356.4 us)
Async XLA Ops:
  7.2 232.4 %copy-start = (bf16[1024,640]{1,0:T(8,128)(2,1)S(1)}, bf16[1024,640]{1,0:T(8,128)(2,1)}, u32[]{:S(2)}) copy-start(bf16[1024,640]{1,0:T(8,128)(2,1)} %param.28) | copy-start | bytes 3932164
  7.2 215.1 %all-reduce.20.cloned.1.call-start = ((), (), s32[]{:S(2)}) async-start(), calls=%async_computation.5 | async-start | bytes 7864320 | tf_op jit(solution)/shard_map/psum | solution.py:176
  10.7 27.1 %copy-start.55 = (f32[640]{0:T(1024)}, f32[640]{0:T(1024)S(1)}, u32[]{:S(2)}) copy-start(f32[640]{0:T(1024)S(1)} %broadcast_add_fusion.4) | copy-start | bytes 7684
  12.7 25.1 %copy-start.53 = (f32[1536]{0:T(1024)}, f32[1536]{0:T(1024)S(1)}, u32[]{:S(2)}) copy-start(f32[1536]{0:T(1024)S(1)} %add_rsqrt_fusion.5) | copy-start | bytes 18436
  116.6 230.7 %all-reduce.22.cloned.1.call-start = ((), (), s32[]{:S(2)}) async-start(), calls=%async_computation.6 | async-start | bytes 7864320 | tf_op jit(solution)/shard_map/psum | solution.py:185
  244.2 105.7 %copy-start.21 = (bf16[1536,640]{1,0:T(8,128)(2,1)S(1)}, bf16[1536,640]{1,0:T(8,128)(2,1)}, u32[]{:S(2)}) copy-start(bf16[1536,640]{1,0:T(8,128)(2,1)} %param.35) | copy-start | bytes 5898244
  244.2 231.3 %all-reduce.24.cloned.1.call-start = ((), (), s32[]{:S(2)}) async-start(), calls=%async_computation.7 | async-start | bytes 7864320 | tf_op jit(solution)/shard_map/psum | solution.py:200
  372.5 323.2 %reduce-scatter.8.cloned.1.call-start = ((), (), s32[]{:S(2)}) async-start(), calls=%async_computation.10 | async-start | bytes 1392640 | tf_op jit(solution)/shard_map/reduce_scatter | solution.py:287
  554.1 12.5 copy-start.40
  593.0 12.5 copy-start.40
  625.9 120.1 %reduce-scatter.6.cloned.1.call-start = ((), (), s32[]{:S(2)}) async-start(), calls=%async_computation.8 | async-start | bytes 1392640 | tf_op jit(solution)/shard_map/reduce_scatter | solution.py:286
  676.1 137.4 %reduce-scatter.14.cloned.1.call-start = ((), (), s32[]{:S(2)}) async-start(), calls=%async_computation.16 | async-start | bytes 2785280 | tf_op jit(solution)/shard_map/reduce_scatter | solution.py:290
  683.0 198.2 %reduce-scatter.12.cloned.1.call-start = ((), (), s32[]{:S(2)}) async-start(), calls=%async_computation.14 | async-start | bytes 2785280 | tf_op jit(solution)/shard_map/reduce_scatter | solution.py:289
  689.3 259.6 %reduce-scatter.10.cloned.1.call-start = ((), (), s32[]{:S(2)}) async-start(), calls=%async_computation.12 | async-start | bytes 2785280 | tf_op jit(solution)/shard_map/reduce_scatter | solution.py:288
  695.6 256.4 %copy-start.45 = (bf16[640,512]{1,0:T(8,128)(2,1)S(1)}, bf16[640,512]{1,0:T(8,128)(2,1)}, u32[]{:S(2)}) copy-start(bf16[640,512]{1,0:T(8,128)(2,1)} %param.22) | copy-start | bytes 1966084
  695.6 293.7 %all-gather.8.cloned.1.call-start = ((), (), s32[]{:S(2)}) async-start(), calls=%async_computation.11 | async-start | bytes 1392640 | tf_op jit(solution)/shard_map/all_gather | solution.py:299
  696.4 333.0 %all-gather.6.cloned.1.call-start = ((), (), s32[]{:S(2)}) async-start(), calls=%async_computation.9 | async-start | bytes 1392640 | tf_op jit(solution)/shard_map/all_gather | solution.py:298
  746.0 328.0 %all-gather.14.cloned.1.call-start = ((), (), s32[]{:S(2)}) async-start(), calls=%async_computation.17 | async-start | bytes 2785280 | tf_op jit(solution)/shard_map/all_gather | solution.py:302
  813.5 304.8 %all-gather.12.cloned.1.call-start = ((), (), s32[]{:S(2)}) async-start(), calls=%async_computation.15 | async-start | bytes 2785280 | tf_op jit(solution)/shard_map/all_gather | solution.py:301
  881.2 281.5 %all-gather.10.cloned.1.call-start = ((), (), s32[]{:S(2)}) async-start(), calls=%async_computation.13 | async-start | bytes 2785280 | tf_op jit(solution)/shard_map/all_gather | solution.py:300
  949.0 386.6 %all-reduce.28.cloned.1.call-start = ((), (), s32[]{:S(2)}) async-start(), calls=%async_computation.19 | async-start | bytes 14155776 | tf_op jit(solution)/shard_map/psum | solution.py:261
  956.8 378.8 %copy-start.26 = (f32[1536,128]{0,1:T(8,128)S(1)}, f32[1536,128]{0,1:T(8,128)}, u32[]{:S(2)}) copy-start(f32[1536,128]{0,1:T(8,128)} %copy-done.25) | copy-start | bytes 2359300
  956.8 570.6 %all-reduce.26.cloned.1.call-start = ((), (), s32[]{:S(2)}) async-start(), calls=%async_computation.18 | async-start | bytes 2621440 | tf_op jit(solution)/shard_map/psum | solution.py:278
  1501.2 31.7 %copy-start.39 = (f32[512,640]{1,0:T(8,128)S(1)}, f32[512,640]{1,0:T(8,128)}, u32[]{:S(2)}) copy-start(f32[512,640]{1,0:T(8,128)} %all-gather.8.cloned.1.call-done) | copy-start | bytes 3932164
  (82 other events, 326.1 us)
Sparse Core Ops, SparseCore 0:
  116.7 105.5 all-reduce.19
  244.3 102.8 all-reduce.21
  372.6 102.8 all-reduce.23
  626.0 58.4 reduce-scatter.7
  688.5 57.4 reduce-scatter.5
  750.6 62.8 reduce-scatter.13
  818.3 62.8 reduce-scatter.11
  886.0 62.8 reduce-scatter.9
  951.5 37.8 all-gather.7
  991.7 37.6 all-gather.5
  1031.9 42.0 all-gather.13
  1076.4 41.8 all-gather.11
  1120.8 41.8 all-gather.9
  1166.0 169.5 all-reduce.27
  1437.1 90.2 all-reduce.25
where the time goes:
time: 1550 us
  waiting for transfers between devices  962 us (62%)
  matrix products  203 us (13%)
  other arithmetic  126 us (8%)
  blocking collectives  124 us (8%)
  local copies, waits for them, and re-layouts  101 us (7%)
  between operations  17.6 us (1%)
    psum x1, waiting for transfers between devices, local(): lax.psum((grad_keys_part, grad_values_part, right_dot(grad_query_low, w_q...  173 us
    unnamed x2, blocking collectives  119 us
    psum x1, waiting for transfers between devices, local(): lax.psum(jnp.dot(mixed_heads, w_output, preferred_element_type=jnp.float3...  105 us
    psum x1, waiting for transfers between devices, local(): lax.psum(jnp.dot(hidden, w_down, preferred_element_type=jnp.float32), 'te...  102 us
    psum x1, waiting for transfers between devices, local(): lax.psum(right_dot(grad_gate_low, w_gate) + right_dot(grad_up_low, w_up),...  100 us
    reduce_scatter x1, waiting for transfers between devices, local(): lax.psum_scatter(grad_up, 'dp', scatter_dimension=0, tiled=True)  67.7 us
    reduce_scatter x1, waiting for transfers between devices, local(): lax.psum_scatter(grad_gate, 'dp', scatter_dimension=0, tiled=True)  67.6 us
    reduce_scatter x1, waiting for transfers between devices, local(): lax.psum_scatter(grad_down, 'dp', scatter_dimension=0, tiled=True)  67.4 us
  transfers between devices with their start and end apart: 15, of which 14 were waited for; matrix products, arithmetic and copies ran while one was open for 5% of the time, Pallas kernels for 0%

commit v1 on v0

--- a/solution.py
+++ b/solution.py
@@ -197,8 +197,9 @@
     grad_up_low = (grad_hidden * activation).astype(jnp.bfloat16)
     grad_gate = left_dot(normed2_low, grad_gate_low)
     grad_up = left_dot(normed2_low, grad_up_low)
-    grad_normed2 = lax.psum(
-        right_dot(grad_gate_low, w_gate) + right_dot(grad_up_low, w_up), "tensor"
+    grad_normed2 = jnp.sum(
+        lax.all_gather(right_dot(grad_gate_low, w_gate) + right_dot(grad_up_low, w_up), "tensor"),
+        axis=0,
     )
     grad_pre_part, grad_pre_ffn = norm_backward(
         grad_normed2, normed2_plain, normed2_inverse, gain_pre_ffn

time: 1550 us -> 1400 us (0.903)
  waiting for transfers between devices: 962 us -> 811 us
    psum x1 -> x0, waiting for transfers between devices: 100 us -> none  [local(): lax.psum(right_dot(grad_gate_low, w_gate) + right_dot(grad_up_low, w_up),...]
    all_gather x0 -> x1, waiting for transfers between devices: none -> 75 us  [local(): lax.all_gather(right_dot(grad_gate_low, w_gate) + right_dot(grad_up_low,...]
    reduce_scatter x1, waiting for transfers between devices: 67.7 us -> 0.02 us  [local(): lax.psum_scatter(grad_up, 'dp', scatter_dimension=0, tiled=True)]
    reduce_scatter x1, waiting for transfers between devices: 67.4 us -> 0.02 us  [local(): lax.psum_scatter(grad_down, 'dp', scatter_dimension=0, tiled=True)]
    reduce_scatter x1, waiting for transfers between devices: 67.6 us -> 3.64 us  [local(): lax.psum_scatter(grad_gate, 'dp', scatter_dimension=0, tiled=True)]
    reduce_scatter x1, waiting for transfers between devices: 0.02 us -> 61.6 us  [local(): lax.psum_scatter(grad_output, 'dp', scatter_dimension=0, tiled=True)]
    unnamed x170 -> x166, local copies, waits for them, and re-layouts: 37.3 us -> 36.8 us
  transfers between devices with their start and end apart: 15 -> 15, of which waited for: 14 -> 13; matrix products, arithmetic and copies ran while one was open for 5% -> 16% of each run, Pallas kernels for 0% -> 0%
where the time goes in v1:
time: 1400 us; the launch traced here: 1390 us
  waiting for transfers between devices  811 us (58%)
  matrix products  204 us (15%)
  blocking collectives  124 us (9%)
  other arithmetic  120 us (9%)
  local copies, waits for them, and re-layouts  104 us (7%)
  between operations  17.7 us (1%)
    psum x1, waiting for transfers between devices, local(): lax.psum((grad_keys_part, grad_values_part, right_dot(grad_query_low, w_q...  173 us
    unnamed x2, blocking collectives  119 us
    psum x1, waiting for transfers between devices, local(): lax.psum(jnp.dot(mixed_heads, w_output, preferred_element_type=jnp.float3...  105 us
    psum x1, waiting for transfers between devices, local(): lax.psum(jnp.dot(hidden, w_down, preferred_element_type=jnp.float32), 'te...  102 us
    all_gather x1, waiting for transfers between devices, local(): lax.all_gather(right_dot(grad_gate_low, w_gate) + right_dot(grad_up_low,...  75 us
    reduce_scatter x1, waiting for transfers between devices, local(): lax.psum_scatter(grad_query, 'dp', scatter_dimension=0, tiled=True)  62 us
    reduce_scatter x1, waiting for transfers between devices, local(): lax.psum_scatter(grad_output, 'dp', scatter_dimension=0, tiled=True)  61.6 us
    all_gather x1, waiting for transfers between devices, local(): lax.all_gather(all_summed[2], 'dp', axis=0, tiled=True)  44.2 us
  transfers between devices with their start and end apart: 15, of which 13 were waited for; matrix products, arithmetic and copies ran while one was open for 16% of the time, Pallas kernels for 0%

profile of v1, /device:TPU:0, one launch (start us, length us, event | category | flops | bytes accessed | tf_op | source)
XLA Modules:
  0.0 1393.5 jit_solution(11422838358714941327)
XLA Ops:
  69.3 39.2 %while.29 = (s32[]{:T(128)}, bf16[3,512,2,256]{3,1,2,0:T(8,128)(2,1)}, f32[3,2,512]{2,1,0:T(2,128)S(1)}, s32[3]{0:T(128)S(1)}, s32[1536]{0:T(1024)S(1)}, /*index...) while((s32[]{:T(128)}, ...), condition=%wide.region_9.10_spmd.clone, body=%wide.region_6.9_spmd.sunk.clone | while | flops 1634205696 | bytes 40944880 | solution.py:174
  117.2 105.1 %all-reduce.19.cloned.1.call-done = f32[1536,640]{1,0:T(8,128)} async-done(((f32[1536,640]{1,0:T(8,128)}), f32[1536,640]{1,0:T(8,128)}) %all-reduce.19.cloned.1.call-update) | async-done | bytes 3932176 | tf_op jit(solution)/shard_map/psum | solution.py:176
  244.7 102.4 %all-reduce.21.cloned.1.call-done = f32[1536,640]{1,0:T(8,128)} async-done(((f32[1536,640]{1,0:T(8,128)}), f32[1536,640]{1,0:T(8,128)}) %all-reduce.21.cloned.1.call-update) | async-done | bytes 3932176 | tf_op jit(solution)/shard_map/psum | solution.py:185
  395.7 75.0 %all-gather.18.cloned.1.call-done = f32[3072,640]{1,0:T(8,128)} async-done(((f32[1536,640]{1,0:T(8,128)}), f32[3072,640]{1,0:T(8,128)}) %all-gather.18.cloned.1.call-update) | async-done | bytes 7864336 | tf_op jit(solution)/shard_map/all_gather | solution.py:201
  496.9 118.3 %while.30 = (s32[]{:T(128)}, f32[1536,256]{1,0:T(8,128)}, f32[1536,256]{1,0:T(8,128)S(1)}, f32[3,512,2,256]{3,1,2,0:T(8,128)}, s32[3]{0:T(128)S(1)}, /*index=5*/...) while((s32[]{:T(128)}, f32[1536,256]{1,0:T(8,128)}, ...), condition=%wide.region_21.22_spmd.clone.clone, body=%wide.region_19.21_spmd.clone.sunk.clone | while | flops 4054849536 | bytes 115111200 | solution.py:247
  513.1 12.3 fusion.188
  525.3 10.7 fusion.190
  551.7 13.5 fusion.188
  565.2 11.0 fusion.190
  592.0 12.6 fusion.188
  604.6 10.7 fusion.190
  635.8 10.9 multiply_reduce_fusion.9
  672.8 61.6 %reduce-scatter.8.cloned.1.call-done = f32[32,640]{1,0:T(8,128)} async-done(((f32[512,640]{1,0:T(8,128)}), f32[32,640]{1,0:T(8,128)}) %reduce-scatter.8.cloned.1.call-update) | async-done | bytes 81936 | tf_op jit(solution)/shard_map/reduce_scatter | solution.py:288
  734.5 62.0 %reduce-scatter.6.cloned.1.call-done = f32[40,512]{1,0:T(8,128)} async-done(((f32[640,512]{1,0:T(8,128)}), f32[40,512]{1,0:T(8,128)}) %reduce-scatter.6.cloned.1.call-update) | async-done | bytes 81936 | tf_op jit(solution)/shard_map/reduce_scatter | solution.py:287
  808.2 32.7 %all-gather.16.cloned.1.call-done = f32[1024,640]{1,0:T(8,128)} async-done(((f32[64,640]{1,0:T(8,128)}), f32[1024,640]{1,0:T(8,128)}) %all-gather.16.cloned.1.call-update) | async-done | bytes 2621456 | tf_op jit(solution)/shard_map/all_gather | solution.py:303
  840.9 44.0 %all-gather.14.cloned.1.call-done = f32[640,1024]{1,0:T(8,128)} async-done(((f32[40,1024]{1,0:T(8,128)}), f32[640,1024]{1,0:T(8,128)}) %all-gather.14.cloned.1.call-update) | async-done | bytes 2621456 | tf_op jit(solution)/shard_map/all_gather | solution.py:302
  884.9 44.2 %all-gather.12.cloned.1.call-done = f32[640,1024]{1,0:T(8,128)} async-done(((f32[40,1024]{1,0:T(8,128)}), f32[640,1024]{1,0:T(8,128)}) %all-gather.12.cloned.1.call-update) | async-done | bytes 2621456 | tf_op jit(solution)/shard_map/all_gather | solution.py:301
  929.1 39.6 %all-gather.10.cloned.1.call-done = f32[512,640]{1,0:T(8,128)} async-done(((f32[32,640]{1,0:T(8,128)}), f32[512,640]{1,0:T(8,128)}) %all-gather.10.cloned.1.call-update) | async-done | bytes 1310736 | tf_op jit(solution)/shard_map/all_gather | solution.py:300
  968.7 39.9 %all-gather.8.cloned.1.call-done = f32[640,512]{1,0:T(8,128)} async-done(((f32[40,512]{1,0:T(8,128)}), f32[640,512]{1,0:T(8,128)}) %all-gather.8.cloned.1.call-update) | async-done | bytes 1310736 | tf_op jit(solution)/shard_map/all_gather | solution.py:299
  1008.7 172.8 %all-reduce.25.cloned.1.call-done = (f32[1536,640]{1,0:T(8,128)}, f32[1536,256]{0,1:T(8,128)}, f32[1536,256]{1,0:T(8,128)}) async-done(((f32[1536,640]{1,0:T(8,128)}, f32[1536,256]{0,1:T(8,128)}, f32[1536,256]{1,0:T(8,128)}), (f32[1536,640]{1,0:T(8,128)}, f32[1536,256]{0,1:T(8,128)}, f32[1536,256]{1,0:T(8,128)})) %all-reduce.25.cloned.1.call-update) | async-done | bytes 7077904 | tf_op jit(solution)/shard_map/psum | solution.py:262
  1207.8 8.9 fusion.65
  1216.6 61.2 %all-reduce.11 = (f32[640]{0:T(1024)S(1)}, f32[256]{0:T(256)S(1)}, f32[640]{0:T(1024)S(1)}, f32[640]{0:T(1024)S(1)}, f32[640]{0:T(1024)S(1)}) all-reduce(f32[640]{0:T(1024)S(1)} %get-tuple-element.261, f32[256]{0:T(256)S(1)} %get-tuple-element.257, ...), channel_id=8, replica_groups=mesh['dp'=16,'tensor'=2] {'dp'}, use_global_device_ids=true, to_apply=%region_36.37.clone | all-reduce | flops 2816 | bytes 22528
  1283.7 58.3 %all-reduce.10 = (f32[640]{0:T(1024)}, f32[256]{0:T(256)}, f32[256]{0:T(256)}, f32[640]{0:T(1024)}, f32[640]{0:T(1024)}, /*index=5*/f32[640]{0:T(1024)}) all-reduce(f32[640]{0:T(1024)S(1)} %dynamic-slice_dynamic-update-slice_fusion.3, f32[256]{0:T(256)S(1)} %dynamic-update-slice.1, ...), channel_id=1, replica_groups=mesh['dp'=16,'tensor'=2] {'dp'}, use_global_device_ids=true, to_apply=%add | all-reduce | flops 3072 | bytes 24576
  1347.1 26.1 %all-reduce.23.cloned.1.call-done = (f32[640,256]{1,0:T(8,128)}, f32[640,256]{1,0:T(8,128)}) async-done(((f32[640,256]{1,0:T(8,128)}, f32[640,256]{1,0:T(8,128)}), (f32[640,256]{1,0:T(8,128)}, f32[640,256]{1,0:T(8,128)})) %all-reduce.23.cloned.1.call-update) | async-done | bytes 1310736 | tf_op jit(solution)/shard_map/psum | solution.py:279
  (388 shorter events, 347.6 us)
Async XLA Ops:
  7.2 232.3 %copy-start = (bf16[1024,640]{1,0:T(8,128)(2,1)S(1)}, bf16[1024,640]{1,0:T(8,128)(2,1)}, u32[]{:S(2)}) copy-start(bf16[1024,640]{1,0:T(8,128)(2,1)} %param.28) | copy-start | bytes 3932164
  7.2 215.0 %all-reduce.19.cloned.1.call-start = ((), (), s32[]{:S(2)}) async-start(), calls=%async_computation.5 | async-start | bytes 7864320 | tf_op jit(solution)/shard_map/psum | solution.py:176
  10.7 27.0 %copy-start.54 = (f32[640]{0:T(1024)}, f32[640]{0:T(1024)S(1)}, u32[]{:S(2)}) copy-start(f32[640]{0:T(1024)S(1)} %broadcast_add_fusion.4) | copy-start | bytes 7684
  12.7 24.9 %copy-start.52 = (f32[1536]{0:T(1024)}, f32[1536]{0:T(1024)S(1)}, u32[]{:S(2)}) copy-start(f32[1536]{0:T(1024)S(1)} %add_rsqrt_fusion.5) | copy-start | bytes 18436
  116.5 230.7 %all-reduce.21.cloned.1.call-start = ((), (), s32[]{:S(2)}) async-start(), calls=%async_computation.6 | async-start | bytes 7864320 | tf_op jit(solution)/shard_map/psum | solution.py:185
  244.1 105.7 %copy-start.19 = (bf16[1536,640]{1,0:T(8,128)(2,1)S(1)}, bf16[1536,640]{1,0:T(8,128)(2,1)}, u32[]{:S(2)}) copy-start(bf16[1536,640]{1,0:T(8,128)(2,1)} %param.35) | copy-start | bytes 5898244
  244.1 226.5 %all-gather.18.cloned.1.call-start = ((), (), s32[]{:S(2)}) async-start(), calls=%async_computation.17 | async-start | bytes 11796480 | tf_op jit(solution)/shard_map/all_gather | solution.py:201
  372.4 295.5 %reduce-scatter.14.cloned.1.call-start = ((), (), s32[]{:S(2)}) async-start(), calls=%async_computation.15 | async-start | bytes 2785280 | tf_op jit(solution)/shard_map/reduce_scatter | solution.py:291
  379.2 289.3 %reduce-scatter.12.cloned.1.call-start = ((), (), s32[]{:S(2)}) async-start(), calls=%async_computation.13 | async-start | bytes 2785280 | tf_op jit(solution)/shard_map/reduce_scatter | solution.py:290
  385.6 287.1 %reduce-scatter.10.cloned.1.call-start = ((), (), s32[]{:S(2)}) async-start(), calls=%async_computation.11 | async-start | bytes 2785280 | tf_op jit(solution)/shard_map/reduce_scatter | solution.py:289
  395.6 338.9 %reduce-scatter.8.cloned.1.call-start = ((), (), s32[]{:S(2)}) async-start(), calls=%async_computation.9 | async-start | bytes 1392640 | tf_op jit(solution)/shard_map/reduce_scatter | solution.py:288
  551.7 13.5 copy-start.39
  592.0 12.6 copy-start.39
  635.7 160.9 %reduce-scatter.6.cloned.1.call-start = ((), (), s32[]{:S(2)}) async-start(), calls=%async_computation.7 | async-start | bytes 1392640 | tf_op jit(solution)/shard_map/reduce_scatter | solution.py:287
  667.7 131.9 %copy-start.44 = (bf16[640,512]{1,0:T(8,128)(2,1)S(1)}, bf16[640,512]{1,0:T(8,128)(2,1)}, u32[]{:S(2)}) copy-start(bf16[640,512]{1,0:T(8,128)(2,1)} %param.22) | copy-start | bytes 1966084
  667.8 173.1 %all-gather.16.cloned.1.call-start = ((), (), s32[]{:S(2)}) async-start(), calls=%async_computation.16 | async-start | bytes 2785280 | tf_op jit(solution)/shard_map/all_gather | solution.py:303
  668.5 216.4 %all-gather.14.cloned.1.call-start = ((), (), s32[]{:S(2)}) async-start(), calls=%async_computation.14 | async-start | bytes 2785280 | tf_op jit(solution)/shard_map/all_gather | solution.py:302
  669.1 260.0 %all-gather.12.cloned.1.call-start = ((), (), s32[]{:S(2)}) async-start(), calls=%async_computation.12 | async-start | bytes 2785280 | tf_op jit(solution)/shard_map/all_gather | solution.py:301
  672.8 296.0 %all-gather.10.cloned.1.call-start = ((), (), s32[]{:S(2)}) async-start(), calls=%async_computation.10 | async-start | bytes 1392640 | tf_op jit(solution)/shard_map/all_gather | solution.py:300
  734.5 274.2 %all-gather.8.cloned.1.call-start = ((), (), s32[]{:S(2)}) async-start(), calls=%async_computation.8 | async-start | bytes 1392640 | tf_op jit(solution)/shard_map/all_gather | solution.py:299
  796.6 384.9 %all-reduce.25.cloned.1.call-start = ((), (), s32[]{:S(2)}) async-start(), calls=%async_computation.19 | async-start | bytes 14155776 | tf_op jit(solution)/shard_map/psum | solution.py:262
  804.4 377.1 %copy-start.23 = (f32[1536,128]{0,1:T(8,128)S(1)}, f32[1536,128]{0,1:T(8,128)}, u32[]{:S(2)}) copy-start(f32[1536,128]{0,1:T(8,128)} %copy-done.22) | copy-start | bytes 2359300
  804.4 568.8 %all-reduce.23.cloned.1.call-start = ((), (), s32[]{:S(2)}) async-start(), calls=%async_computation.18 | async-start | bytes 2621440 | tf_op jit(solution)/shard_map/psum | solution.py:279
  1347.1 31.6 %copy-start.38 = (f32[512,640]{1,0:T(8,128)S(1)}, f32[512,640]{1,0:T(8,128)}, u32[]{:S(2)}) copy-start(f32[512,640]{1,0:T(8,128)} %all-gather.10.cloned.1.call-done) | copy-start | bytes 3932164
  (80 other events, 323.9 us)
Sparse Core Ops, SparseCore 0:
  116.6 105.6 all-reduce.18
  244.2 102.8 all-reduce.20
  372.5 98.0 all-gather.17
  474.8 63.8 reduce-scatter.13
  542.9 62.7 reduce-scatter.11
  609.9 62.8 reduce-scatter.9
  677.0 57.4 reduce-scatter.7
  739.1 57.4 reduce-scatter.5
  798.8 41.9 all-gather.15
  843.0 41.8 all-gather.13
  887.2 41.8 all-gather.11
  931.2 37.4 all-gather.9
  971.0 37.6 all-gather.7
  1011.7 169.7 all-reduce.24
  1282.9 90.2 all-reduce.22
